TPU v7x, 32 devices: a whole 2x2x4 slice. The times are simulated.
32 devices in a mesh: parts: 2 (over y), wide: 8 (over z, x), narrow: 2 (over core).
Axes of the slice: x: 2, y: 2, z: 4, core: 2. Of those that a mesh axis runs over, the one named last changes fastest.
Arguments:
- signal: bfloat16 [4096, 768], P(('parts', 'wide', 'narrow')), parts along dimension 0, may hold values from -6 to 6
- gate_values: bfloat16 [4096, 768], P(('parts', 'wide', 'narrow')), parts along dimension 0, may hold values from -6 to 6
- filter_taps: bfloat16 [2048, 768], P(('wide', 'narrow')), may hold values from -1.1 to 1.1
- skip_gain: float32 [768], P(('wide', 'narrow')), may hold values from -4 to 4
- grad_output: bfloat16 [4096, 768], P(('parts', 'wide', 'narrow')), parts along dimension 0, may hold values from -6 to 6
Outputs:
- signal_grad: bfloat16 [4096, 768], P(('parts', 'wide', 'narrow')), parts along dimension 0
- gate_grad: bfloat16 [4096, 768], P(('parts', 'wide', 'narrow')), parts along dimension 0
- filter_grad: bfloat16 [4096, 768], P(('parts', 'wide', 'narrow')), parts along dimension 0
There are 2 independent parts, one for each index of `parts`. A program takes and returns all parts, laid end to end along the dimension named above; an argument that names none is the same for every part. Nothing has to cross between parts.
All inputs are finite; a program needn't handle non-finite values.
Results may differ from a plain program's by a relative error of at most 0.0051.
Values may be sent and summed in bfloat16 or wider, within the bound.
A program may use at most 64 MiB of HBM per device.

v0:
```python
import functools
import math

import jax
import jax.numpy as jnp
import numpy as np
from jax import lax
from jax.experimental import pallas as pl
from jax.experimental.pallas import tpu as pltpu
from jax.sharding import PartitionSpec as P

precise = lax.Precision.HIGHEST


def angle_tables(left_count, right_count, period):
    left_index = jnp.arange(left_count, dtype=jnp.int32)
    right_index = jnp.arange(right_count, dtype=jnp.int32)
    phases = left_index[:, None] * right_index[None, :] % period
    angles = phases.astype(jnp.float32) * (2.0 * math.pi / period)
    return (jnp.cos(angles), jnp.sin(angles))


def spectral_tables(groups, seq_rows):
    full_span = 2 * groups * seq_rows
    outer_cos, outer_sin = angle_tables(2 * groups, groups, 2 * groups)
    twist_cos, twist_sin = angle_tables(2 * groups, seq_rows, full_span)
    inner_cos, inner_sin = angle_tables(seq_rows, seq_rows, seq_rows)
    return (outer_cos, outer_sin, twist_cos, twist_sin, inner_cos, inner_sin, full_span)


def transform(field, tables):
    outer_cos, outer_sin, twist_cos, twist_sin, inner_cos, inner_sin, full_span = tables
    first_real = jnp.einsum("ka,ucab->uckb", outer_cos, field, precision=precise)
    first_imag = -jnp.einsum("ka,ucab->uckb", outer_sin, field, precision=precise)
    turned_real = first_real * twist_cos + first_imag * twist_sin
    turned_imag = first_imag * twist_cos - first_real * twist_sin
    spec_real = jnp.einsum("uckb,bj->uckj", turned_real, inner_cos, precision=precise) + jnp.einsum(
        "uckb,bj->uckj", turned_imag, inner_sin, precision=precise
    )
    spec_imag = jnp.einsum("uckb,bj->uckj", turned_imag, inner_cos, precision=precise) - jnp.einsum(
        "uckb,bj->uckj", turned_real, inner_sin, precision=precise
    )
    return (spec_real, spec_imag)


def untwist(spec_real, spec_imag, tables):
    outer_cos, outer_sin, twist_cos, twist_sin, inner_cos, inner_sin, full_span = tables
    back_real = jnp.einsum("uckj,bj->uckb", spec_real, inner_cos, precision=precise) - jnp.einsum(
        "uckj,bj->uckb", spec_imag, inner_sin, precision=precise
    )
    back_imag = jnp.einsum("uckj,bj->uckb", spec_imag, inner_cos, precision=precise) + jnp.einsum(
        "uckj,bj->uckb", spec_real, inner_sin, precision=precise
    )
    turned_real = back_real * twist_cos - back_imag * twist_sin
    turned_imag = back_imag * twist_cos + back_real * twist_sin
    return (turned_real, turned_imag)


def inverse_real(spec_real, spec_imag, tables):
    outer_cos, outer_sin = (tables[0], tables[1])
    factor = 1.0 / tables[6]
    turned_real, turned_imag = untwist(spec_real, spec_imag, tables)
    out_real = jnp.einsum("ka,uckb->ucab", outer_cos, turned_real, precision=precise) - jnp.einsum(
        "ka,uckb->ucab", outer_sin, turned_imag, precision=precise
    )
    return out_real * factor


def to_channels(stacked, wide_count, narrow_count):
    stack_count, channels, seq_rows = stacked.shape
    groups = wide_count * narrow_count
    own_channels = channels // groups
    arrived = lax.all_to_all(stacked, ("wide", "narrow"), split_axis=1, concat_axis=2, tiled=True)
    return arrived.reshape(stack_count, own_channels, groups, seq_rows)


def to_sequence(field):
    stack_count, own_channels, groups, seq_rows = field.shape
    flat_field = field.reshape(stack_count, own_channels, groups * seq_rows)
    arrived = lax.all_to_all(
        flat_field, ("wide", "narrow"), split_axis=2, concat_axis=1, tiled=True
    )
    return arrived


def backward_channels(
    inner_chan,
    inner_real,
    inner_imag,
    signal_real,
    signal_imag,
    taps_real,
    taps_imag,
    skip_gain,
    tables,
    total_rows,
):
    taps_side_real = inner_real * taps_real + inner_imag * taps_imag
    taps_side_imag = inner_imag * taps_real - inner_real * taps_imag
    signal_side_real = inner_real * signal_real + inner_imag * signal_imag
    signal_side_imag = inner_imag * signal_real - inner_real * signal_imag
    back_taps = inverse_real(taps_side_real, taps_side_imag, tables)
    back_signal = inverse_real(signal_side_real, signal_side_imag, tables)
    signal_chan = (back_taps[0] + skip_gain[:, None, None] * inner_chan[0]).astype(jnp.bfloat16)
    filter_chan = (back_signal[0] * (1.0 / math.sqrt(total_rows))).astype(jnp.bfloat16)
    return (signal_chan, filter_chan)


def per_device_plain(signal, gate_values, filter_taps, skip_gain, grad_output):
    wide_count = lax.axis_size("wide")
    narrow_count = lax.axis_size("narrow")
    groups = wide_count * narrow_count
    seq_rows = signal.shape[0]
    total_rows = groups * seq_rows
    tables = spectral_tables(groups, seq_rows)
    grad_vals = grad_output.astype(jnp.float32)
    paired = jnp.stack([jnp.transpose(signal), jnp.transpose(filter_taps)])
    spread_pair = to_channels(paired, wide_count, narrow_count).astype(jnp.float32)
    pair_real, pair_imag = transform(spread_pair, tables)
    signal_real, signal_imag = (pair_real[0:1], pair_imag[0:1])
    taps_real, taps_imag = (pair_real[1:2], pair_imag[1:2])
    conv_real = signal_real * taps_real - signal_imag * taps_imag
    conv_imag = signal_real * taps_imag + signal_imag * taps_real
    convolved = inverse_real(conv_real, conv_imag, tables)[0]
    mixed_chan = (convolved + skip_gain[:, None, None] * spread_pair[0]).astype(jnp.bfloat16)
    mixed_rows = jnp.transpose(to_sequence(mixed_chan[None])[0])
    gate_grad = (grad_vals * mixed_rows.astype(jnp.float32)).astype(jnp.bfloat16)
    inner_grad = (grad_vals * gate_values.astype(jnp.float32)).astype(jnp.bfloat16)
    inner_chan = to_channels(jnp.transpose(inner_grad)[None], wide_count, narrow_count).astype(
        jnp.float32
    )
    inner_real, inner_imag = transform(inner_chan, tables)
    signal_chan, filter_chan = backward_channels(
        inner_chan,
        inner_real,
        inner_imag,
        signal_real,
        signal_imag,
        taps_real,
        taps_imag,
        skip_gain,
        tables,
        total_rows,
    )
    returned = to_sequence(jnp.stack([signal_chan, filter_chan]))
    signal_grad = jnp.transpose(returned[0])
    filter_grad = jnp.transpose(returned[1])
    return (signal_grad, gate_grad, filter_grad)


LANES = 128
CHUNK = 16
MESH = pl.DeviceIdType.MESH


def fused_tables(groups, seq_rows):
    span = 2 * groups * seq_rows
    kept = np.arange(groups + 1)[:, None]
    turn = 2.0 * np.pi * (kept * np.arange(seq_rows)[None, :]) / span
    weight = np.where((kept == 0) | (kept == groups), 1.0, 2.0) / span
    twist = np.stack([np.cos(turn), np.sin(turn), weight * np.cos(turn), weight * np.sin(turn)])
    index = np.arange(seq_rows)
    angle = 2.0 * np.pi * (index[:, None] * index[None, :] % seq_rows) / seq_rows
    cos, sin = np.cos(angle), np.sin(angle)
    ahead = np.block([[cos, -sin], [sin, cos]]).astype(np.float32)
    both = []
    for table in (ahead, ahead.T):
        high = table.astype(jnp.bfloat16)
        both += [high, (table - high.astype(np.float32)).astype(jnp.bfloat16)]
    return twist.astype(np.float32), np.stack(both)


def weighted_sum(pairs):
    by_size = {}
    for coefficient, array in pairs:
        if abs(coefficient) > 1e-9:
            key = round(abs(coefficient), 9)
            by_size.setdefault(key, (abs(coefficient), []))[1].append((coefficient > 0, array))
    total = None
    for size, members in by_size.values():
        members = sorted(members, key=lambda member: not member[0])
        positive = members[0][0]
        partial = members[0][1]
        for sign, array in members[1:]:
            partial = partial + array if sign == positive else partial - array
        factor = 1.0 if abs(size - 1.0) < 1e-9 else size
        if factor != 1.0:
            partial = partial * np.float32(factor)
        if total is None:
            total = partial if positive else -partial
        else:
            total = total + partial if positive else total - partial
    return total


def add(left, right):
    if left is None or right is None:
        return right if left is None else left
    return left + right


def sub(left, right):
    if left is None:
        return None if right is None else -right
    return left if right is None else left - right


def outer_forward(x):
    groups = len(x)
    half = groups // 2
    unit = math.pi / groups
    plus = {a: x[a] + x[groups - a] for a in range(1, half)}
    minus = {a: x[a] - x[groups - a] for a in range(1, half)}
    real, imag = [None] * (groups + 1), [None] * (groups + 1)
    for k in range(half + 1):
        even = k % 2 == 0
        cos_side, sin_side = (plus, minus) if even else (minus, plus)
        cos_parts, sin_parts = [[(1.0, x[0])], []], [[], []]
        cos_parts[half % 2].append((math.cos(unit * k * half), x[half]))
        sin_parts[half % 2].append((math.sin(unit * k * half), x[half]))
        for a in range(1, half):
            cos_parts[a % 2].append((math.cos(unit * k * a), cos_side[a]))
            sin_parts[a % 2].append((math.sin(unit * k * a), sin_side[a]))
        cos_even, cos_odd = weighted_sum(cos_parts[0]), weighted_sum(cos_parts[1])
        sin_even, sin_odd = weighted_sum(sin_parts[0]), weighted_sum(sin_parts[1])
        real[k] = add(cos_even, cos_odd)
        imag[k] = sub(sub(None, sin_even), sin_odd)
        real[groups - k] = sub(cos_even, cos_odd)
        if k < half:
            imag[groups - k] = sub(sin_even, sin_odd)
    zero = jnp.zeros_like(x[0])
    return [zero if v is None else v for v in real], [zero if v is None else v for v in imag]


def outer_inverse(real, imag):
    groups = len(real) - 1
    half = groups // 2
    unit = math.pi / groups
    out = [None] * groups
    for a_parity in (0, 1):
        cos_side, sin_side = {}, {}
        for k in range(1, half):
            if a_parity == 0:
                cos_side[k] = real[k] + real[groups - k]
                sin_side[k] = imag[k] - imag[groups - k]
            else:
                cos_side[k] = real[k] - real[groups - k]
                sin_side[k] = imag[k] + imag[groups - k]
        ends = real[0] + real[groups] if a_parity == 0 else real[0] - real[groups]
        for a in range(a_parity, half + 1, 2):
            cos_parts, sin_parts = [[(1.0, ends)], []], [[], []]
            cos_parts[half % 2].append((math.cos(unit * half * a), real[half]))
            sin_parts[half % 2].append((math.sin(unit * half * a), imag[half]))
            for k in range(1, half):
                cos_parts[k % 2].append((math.cos(unit * k * a), cos_side[k]))
                sin_parts[k % 2].append((math.sin(unit * k * a), sin_side[k]))
            cos_even, cos_odd = weighted_sum(cos_parts[0]), weighted_sum(cos_parts[1])
            sin_even, sin_odd = weighted_sum(sin_parts[0]), weighted_sum(sin_parts[1])
            out[a] = sub(sub(add(cos_even, cos_odd), sin_even), sin_odd)
            if 0 < a < half:
                out[groups - a] = sub(add(sub(cos_even, cos_odd), sin_even), sin_odd)
    return out


def split(value):
    high = value.astype(jnp.bfloat16)
    return high, (value - high.astype(jnp.float32)).astype(jnp.bfloat16)


def fused_kernel(
    groups,
    narrow_count,
    total_rows,
    signal_ref,
    gate_ref,
    taps_ref,
    skip_ref,
    grad_ref,
    twist_ref,
    inner_ref,
    signal_out,
    gate_out,
    filter_out,
    outgoing,
    arrived,
    results,
    returned,
    high_ref,
    low_ref,
    spec_ref,
    out_send,
    out_recv,
    back_send,
    back_recv,
    local_sem,
):
    seq_rows, channels = signal_ref.shape
    own = channels // groups
    chunks = own // CHUNK
    part = lax.axis_index("parts")
    me = lax.axis_index("wide") * narrow_count + lax.axis_index("narrow")

    def device(index):
        return (part, index // narrow_count, index % narrow_count)

    barrier = pltpu.get_barrier_semaphore()

    def greet(step, carry):
        pl.semaphore_signal(
            barrier, inc=1, device_id=device((me + step) % groups), device_id_type=MESH
        )
        return carry

    lax.fori_loop(1, groups, greet, 0)

    for first in range(0, channels, LANES):
        columns = slice(first, first + LANES)
        grad_vals = grad_ref[:, columns].astype(jnp.float32)
        inner = (grad_vals * gate_ref[:, columns].astype(jnp.float32)).astype(jnp.bfloat16)
        outgoing[0, columns, :] = signal_ref[:, columns].T
        outgoing[1, columns, :] = taps_ref[:, columns].T
        outgoing[2, columns, :] = inner.T
    pl.semaphore_wait(barrier, groups - 1)

    def rows_of(index, chunk):
        return pl.ds(pl.multiple_of(index * own + chunk * CHUNK, CHUNK), CHUNK)

    def chunk_rows(chunk):
        return pl.ds(pl.multiple_of(chunk * CHUNK, CHUNK), CHUNK)

    def spread(chunk, step):
        other = (me + step) % groups
        return pltpu.make_async_remote_copy(
            src_ref=outgoing.at[:, rows_of(other, chunk), :],
            dst_ref=arrived.at[me, :, chunk_rows(chunk), :],
            send_sem=out_send.at[chunk, step],
            recv_sem=out_recv.at[chunk, step],
            device_id=device(other),
            device_id_type=MESH,
        )

    def bring(chunk, step):
        other = (me + step) % groups
        return pltpu.make_async_remote_copy(
            src_ref=results.at[other, :, chunk_rows(chunk), :],
            dst_ref=returned.at[:, rows_of(me, chunk), :],
            send_sem=back_send.at[chunk, step],
            recv_sem=back_recv.at[chunk, step],
            device_id=device(other),
            device_id_type=MESH,
        )

    for chunk in range(chunks):

        def start(step, carry, chunk=chunk):
            spread(chunk, step).start()
            return carry

        lax.fori_loop(1, groups, start, 0)
    keep = pltpu.make_async_copy(
        outgoing.at[:, pl.ds(pl.multiple_of(me * own, CHUNK), own), :],
        arrived.at[me],
        local_sem,
    )
    keep.start()

    lane = lax.broadcasted_iota(jnp.int32, (own, own), 1)
    row = lax.broadcasted_iota(jnp.int32, (own, own), 0)
    gain_all = jnp.sum(
        jnp.where(lane == row, jnp.broadcast_to(skip_ref[...], (own, own)), 0.0),
        axis=1,
        keepdims=True,
    )
    keep.wait()

    kept = groups + 1
    size = kept * 3 * CHUNK

    def inner_transform(which):
        high = high_ref[...].reshape(size, 2 * seq_rows)
        low = low_ref[...].reshape(size, 2 * seq_rows)
        table_high, table_low = inner_ref[which], inner_ref[which + 1]
        dot = functools.partial(jnp.dot, preferred_element_type=jnp.float32)
        total = dot(high, table_high) + dot(high, table_low) + dot(low, table_high)
        spec_ref[...] = total.reshape(kept, 3, CHUNK, 2 * seq_rows)

    def store_pair(k, u, real, imag):
        real_high, real_low = split(real)
        imag_high, imag_low = split(imag)
        high_ref[k, u, :, :seq_rows] = real_high
        high_ref[k, u, :, seq_rows:] = imag_high
        low_ref[k, u, :, :seq_rows] = real_low
        low_ref[k, u, :, seq_rows:] = imag_low

    for chunk in range(chunks):
        rows = slice(chunk * CHUNK, (chunk + 1) * CHUNK)

        def await_in(step, carry, chunk=chunk):
            spread(chunk, step).wait_recv()
            return carry

        lax.fori_loop(1, groups, await_in, 0)

        def ahead(u, carry, rows=rows):
            blocks = [arrived[a, u, rows, :].astype(jnp.float32) for a in range(groups)]
            real, imag = outer_forward(blocks)
            for k in range(kept):
                cos, sin = twist_ref[0, k : k + 1, :], twist_ref[1, k : k + 1, :]
                store_pair(
                    k, u, real[k] * cos + imag[k] * sin, imag[k] * cos - real[k] * sin
                )
            return carry

        lax.fori_loop(0, 3, ahead, 0)
        inner_transform(0)

        def multiply(k, carry):
            parts = [
                (spec_ref[k, u, :, :seq_rows], spec_ref[k, u, :, seq_rows:]) for u in range(3)
            ]
            (s_re, s_im), (t_re, t_im), (i_re, i_im) = parts
            store_pair(k, 0, s_re * t_re - s_im * t_im, s_re * t_im + s_im * t_re)
            store_pair(k, 1, i_re * t_re + i_im * t_im, i_im * t_re - i_re * t_im)
            store_pair(k, 2, i_re * s_re + i_im * s_im, i_im * s_re - i_re * s_im)
            return carry

        lax.fori_loop(0, kept, multiply, 0)
        inner_transform(2)

        gain = gain_all[rows, :]

        def back(u, carry, rows=rows, gain=gain):
            real, imag = [], []
            for k in range(kept):
                re, im = spec_ref[k, u, :, :seq_rows], spec_ref[k, u, :, seq_rows:]
                cos, sin = twist_ref[2, k : k + 1, :], twist_ref[3, k : k + 1, :]
                real.append(re * cos - im * sin)
                imag.append(im * cos + re * sin)
            for a, block in enumerate(outer_inverse(real, imag)):
                skipped = arrived[a, 2 * u, rows, :].astype(jnp.float32)
                results[a, u, rows, :] = (block + gain * skipped).astype(jnp.bfloat16)
            return carry

        lax.fori_loop(0, 2, back, 0)
        real, imag = [], []
        for k in range(kept):
            re, im = spec_ref[k, 2, :, :seq_rows], spec_ref[k, 2, :, seq_rows:]
            cos, sin = twist_ref[2, k : k + 1, :], twist_ref[3, k : k + 1, :]
            real.append(re * cos - im * sin)
            imag.append(im * cos + re * sin)
        for a, block in enumerate(outer_inverse(real, imag)):
            scaled = block * np.float32(1.0 / math.sqrt(total_rows))
            results[a, 2, rows, :] = scaled.astype(jnp.bfloat16)

        def start_back(step, carry, chunk=chunk):
            bring(chunk, step).start()
            return carry

        lax.fori_loop(1, groups, start_back, 0)

    mine = pltpu.make_async_copy(
        results.at[me],
        returned.at[:, pl.ds(pl.multiple_of(me * own, CHUNK), own), :],
        local_sem,
    )
    mine.start()
    mine.wait()
    for chunk in range(chunks):

        def finish(step, carry, chunk=chunk):
            bring(chunk, step).wait_recv()
            return carry

        lax.fori_loop(1, groups, finish, 0)

    for first in range(0, channels, LANES):
        columns = slice(first, first + LANES)
        mixed = returned[0, columns, :].T.astype(jnp.float32)
        gate_out[:, columns] = (grad_ref[:, columns].astype(jnp.float32) * mixed).astype(
            jnp.bfloat16
        )
        signal_out[:, columns] = returned[1, columns, :].T
        filter_out[:, columns] = returned[2, columns, :].T

    for chunk in range(chunks):

        def drain(step, carry, chunk=chunk):
            spread(chunk, step).wait_send()
            bring(chunk, step).wait_send()
            return carry

        lax.fori_loop(1, groups, drain, 0)


def per_device_fused(signal, gate_values, filter_taps, skip_gain, grad_output):
    narrow_count = lax.axis_size("narrow")
    groups = lax.axis_size("wide") * narrow_count
    seq_rows, channels = signal.shape
    own = channels // groups
    chunks = own // CHUNK
    twist, inner = fused_tables(groups, seq_rows)
    vmem = pl.BlockSpec(memory_space=pltpu.VMEM)
    shape = jax.ShapeDtypeStruct((seq_rows, channels), jnp.bfloat16)
    rows = (groups + 1, 3, CHUNK, 2 * seq_rows)
    return pl.pallas_call(
        functools.partial(fused_kernel, groups, narrow_count, groups * seq_rows),
        out_shape=(shape, shape, shape),
        in_specs=[vmem] * 7,
        out_specs=(vmem, vmem, vmem),
        scratch_shapes=[
            pltpu.VMEM((3, channels, seq_rows), jnp.bfloat16),
            pltpu.VMEM((groups, 3, own, seq_rows), jnp.bfloat16),
            pltpu.VMEM((groups, 3, own, seq_rows), jnp.bfloat16),
            pltpu.VMEM((3, channels, seq_rows), jnp.bfloat16),
            pltpu.VMEM(rows, jnp.bfloat16),
            pltpu.VMEM(rows, jnp.bfloat16),
            pltpu.VMEM(rows, jnp.float32),
            pltpu.SemaphoreType.DMA((chunks, groups)),
            pltpu.SemaphoreType.DMA((chunks, groups)),
            pltpu.SemaphoreType.DMA((chunks, groups)),
            pltpu.SemaphoreType.DMA((chunks, groups)),
            pltpu.SemaphoreType.DMA,
        ],
        compiler_params=pltpu.CompilerParams(
            collective_id=0, has_side_effects=True, vmem_limit_bytes=40 * 1024 * 1024
        ),
    )(
        signal,
        gate_values,
        filter_taps,
        skip_gain[None, :],
        grad_output,
        jnp.asarray(twist),
        jnp.asarray(inner),
    )


def per_device(signal, gate_values, filter_taps, skip_gain, grad_output):
    groups = lax.axis_size("wide") * lax.axis_size("narrow")
    seq_rows, channels = signal.shape
    own = channels // groups
    fits = groups <= 32 and groups % 4 == 0 and seq_rows == LANES
    if fits and own >= CHUNK and own % CHUNK == 0 and channels % LANES == 0:
        return per_device_fused(signal, gate_values, filter_taps, skip_gain, grad_output)
    return per_device_plain(signal, gate_values, filter_taps, skip_gain, grad_output)


def solution(mesh):
    placed = (
        P(("parts", "wide", "narrow"), None),
        P(("parts", "wide", "narrow"), None),
        P(("wide", "narrow"), None),
        P(("wide", "narrow")),
        P(("parts", "wide", "narrow"), None),
    )
    return jax.shard_map(
        per_device,
        mesh=mesh,
        in_specs=placed,
        out_specs=(
            P(("parts", "wide", "narrow"), None),
            P(("parts", "wide", "narrow"), None),
            P(("parts", "wide", "narrow"), None),
        ),
        check_vma=False,
    )
```

profile of v0, /device:TPU:0, one launch (start us, length us, event | category | flops | bytes accessed | tf_op | source)
XLA Modules:
  0.0 43.5 jit_solution(16233761399969660937)
XLA Ops:
  0.6 0.0 copy-start.6
  0.6 0.6 %copy-done.6 = f32[48]{0:T(128)S(1)} copy-done((f32[48]{0:T(128)S(1)}, f32[48]{0:T(128)}, u32[]{:S(2)}) %copy-start.6) | copy-done | bytes 216
  1.3 0.0 copy-start
  1.3 1.0 %copy-done = bf16[4,256,256]{2,1,0:T(8,128)(2,1)S(1)} copy-done((bf16[4,256,256]{2,1,0:T(8,128)(2,1)S(1)}, bf16[4,256,256]{2,1,0:T(8,128)(2,1)}, u32[]{:S(2)}) %copy-start) | copy-done | bytes 524312
  2.3 0.0 copy-start.1
  2.3 0.9 %copy-done.1 = bf16[128,768]{1,0:T(8,128)(2,1)S(1)} copy-done((bf16[128,768]{1,0:T(8,128)(2,1)S(1)}, bf16[128,768]{1,0:T(8,128)(2,1)}, u32[]{:S(2)}) %copy-start.1) | copy-done | bytes 196632
  3.3 0.0 copy-start.2
  3.3 0.9 %copy-done.2 = bf16[128,768]{1,0:T(8,128)(2,1)S(1)} copy-done((bf16[128,768]{1,0:T(8,128)(2,1)S(1)}, bf16[128,768]{1,0:T(8,128)(2,1)}, u32[]{:S(2)}) %copy-start.2) | copy-done | bytes 196632
  4.2 0.0 copy-start.3
  4.2 0.9 %copy-done.3 = bf16[128,768]{1,0:T(8,128)(2,1)S(1)} copy-done((bf16[128,768]{1,0:T(8,128)(2,1)S(1)}, bf16[128,768]{1,0:T(8,128)(2,1)}, u32[]{:S(2)}) %copy-start.3) | copy-done | bytes 196632
  5.1 0.0 copy-start.4
  5.1 0.9 %copy-done.4 = bf16[128,768]{1,0:T(8,128)(2,1)S(1)} copy-done((bf16[128,768]{1,0:T(8,128)(2,1)S(1)}, bf16[128,768]{1,0:T(8,128)(2,1)}, u32[]{:S(2)}) %copy-start.4) | copy-done | bytes 196632
  6.0 0.0 copy-start.5
  6.0 0.8 %copy-done.5 = f32[4,17,128]{2,1,0:T(8,128)S(1)} copy-done((f32[4,17,128]{2,1,0:T(8,128)S(1)}, f32[4,17,128]{2,1,0:T(8,128)}, u32[]{:S(2)}) %copy-start.5) | copy-done | bytes 34840
  6.8 34.6 %shard_map.94 = (bf16[128,768]{1,0:T(8,128)(2,1)S(1)}, bf16[128,768]{1,0:T(8,128)(2,1)S(1)}, bf16[128,768]{1,0:T(8,128)(2,1)S(1)}) custom-call(bf16[128,768]{1,0:T(8,128)(2,1)S(1)} %copy-done.1, bf16[128,768]{1,0:T(8,128)(2,1)S(1)} %copy-done.2, bf16[128,768]{1,0:T(8,128)(2,1)S(1)} %copy-done.3, f32[1,48]{1,0:T(1,128)S(1)} %bitcast.1, ...), custom_call_target="tpu_custom_call" | custom-call | tf_op jit(solution)/shard_map/pallas_call | solution.py:505
  41.4 0.7 %copy.13 = bf16[128,768]{1,0:T(8,128)(2,1)} copy(bf16[128,768]{1,0:T(8,128)(2,1)S(1)} %get-tuple-element.6) | data formatting | bytes 393216
  42.1 0.7 %copy.14 = bf16[128,768]{1,0:T(8,128)(2,1)} copy(bf16[128,768]{1,0:T(8,128)(2,1)S(1)} %get-tuple-element.7) | data formatting | bytes 393216
  42.8 0.7 %copy.15 = bf16[128,768]{1,0:T(8,128)(2,1)} copy(bf16[128,768]{1,0:T(8,128)(2,1)S(1)} %get-tuple-element.8) | data formatting | bytes 393216
Async XLA Ops:
  0.6 0.7 %copy-start.6 = (f32[48]{0:T(128)S(1)}, f32[48]{0:T(128)}, u32[]{:S(2)}) copy-start(f32[48]{0:T(128)} %param.10) | copy-start | bytes 580
  1.3 1.0 %copy-start = (bf16[4,256,256]{2,1,0:T(8,128)(2,1)S(1)}, bf16[4,256,256]{2,1,0:T(8,128)(2,1)}, u32[]{:S(2)}) copy-start(bf16[4,256,256]{2,1,0:T(8,128)(2,1)} %constant.5.clone.inner_ref) | copy-start | bytes 1572868
  2.3 0.9 %copy-start.1 = (bf16[128,768]{1,0:T(8,128)(2,1)S(1)}, bf16[128,768]{1,0:T(8,128)(2,1)}, u32[]{:S(2)}) copy-start(bf16[128,768]{1,0:T(8,128)(2,1)} %signal_ref.1) | copy-start | bytes 589828
  3.3 0.9 %copy-start.2 = (bf16[128,768]{1,0:T(8,128)(2,1)S(1)}, bf16[128,768]{1,0:T(8,128)(2,1)}, u32[]{:S(2)}) copy-start(bf16[128,768]{1,0:T(8,128)(2,1)} %gate_ref.1) | copy-start | bytes 589828
  4.2 0.9 %copy-start.3 = (bf16[128,768]{1,0:T(8,128)(2,1)S(1)}, bf16[128,768]{1,0:T(8,128)(2,1)}, u32[]{:S(2)}) copy-start(bf16[128,768]{1,0:T(8,128)(2,1)} %taps_ref.1) | copy-start | bytes 589828
  5.1 0.9 %copy-start.4 = (bf16[128,768]{1,0:T(8,128)(2,1)S(1)}, bf16[128,768]{1,0:T(8,128)(2,1)}, u32[]{:S(2)}) copy-start(bf16[128,768]{1,0:T(8,128)(2,1)} %grad_ref.1) | copy-start | bytes 589828
  6.0 0.8 %copy-start.5 = (f32[4,17,128]{2,1,0:T(8,128)S(1)}, f32[4,17,128]{2,1,0:T(8,128)}, u32[]{:S(2)}) copy-start(f32[4,17,128]{2,1,0:T(8,128)} %constant.4.clone.twist_ref) | copy-start | bytes 104452
where the time goes:
time: 43.8 us; the launch traced here: 43.5 us
  Pallas kernels  34.6 us (79%)
  local copies, waits for them, and re-layouts  8.22 us (19%)
  between operations  0.66 us (2%)
    pallas_call x1, Pallas kernels, per_device_fused(): pl.pallas_call(functools.partial(fused_kernel, groups, narrow_count, grou...  34.6 us
    unnamed x17, local copies, waits for them, and re-layouts  8.22 us

commit v1 on v0

--- a/solution.py
+++ b/solution.py
@@ -271,6 +271,14 @@
     groups,
     narrow_count,
     total_rows,
+    signal_hbm,
+    gate_hbm,
+    taps_hbm,
+    skip_hbm,
+    grad_hbm,
+    twist_hbm,
+    inner_hbm,
+    returned,
     signal_ref,
     gate_ref,
     taps_ref,
@@ -278,13 +286,9 @@
     grad_ref,
     twist_ref,
     inner_ref,
-    signal_out,
-    gate_out,
-    filter_out,
     outgoing,
     arrived,
     results,
-    returned,
     high_ref,
     low_ref,
     spec_ref,
@@ -293,6 +297,7 @@
     back_send,
     back_recv,
     local_sem,
+    load_sem,
 ):
     seq_rows, channels = signal_ref.shape
     own = channels // groups
@@ -304,6 +309,20 @@
         return (part, index // narrow_count, index % narrow_count)
 
     barrier = pltpu.get_barrier_semaphore()
+    pairs = [
+        (signal_hbm, signal_ref),
+        (taps_hbm, taps_ref),
+        (grad_hbm, grad_ref),
+        (gate_hbm, gate_ref),
+        (skip_hbm, skip_ref),
+        (twist_hbm, twist_ref),
+        (inner_hbm, inner_ref),
+    ]
+    loads = [
+        pltpu.make_async_copy(far, near, load_sem.at[i]) for i, (far, near) in enumerate(pairs)
+    ]
+    for load in loads:
+        load.start()
 
     def greet(step, carry):
         pl.semaphore_signal(
@@ -313,6 +332,8 @@
 
     lax.fori_loop(1, groups, greet, 0)
 
+    for load in loads[:4]:
+        load.wait()
     for first in range(0, channels, LANES):
         columns = slice(first, first + LANES)
         grad_vals = grad_ref[:, columns].astype(jnp.float32)
@@ -364,6 +385,8 @@
     )
     keep.start()
 
+    for load in loads[4:]:
+        load.wait()
     lane = lax.broadcasted_iota(jnp.int32, (own, own), 1)
     row = lax.broadcasted_iota(jnp.int32, (own, own), 0)
     gain_all = jnp.sum(
@@ -473,15 +496,6 @@
 
         lax.fori_loop(1, groups, finish, 0)
 
-    for first in range(0, channels, LANES):
-        columns = slice(first, first + LANES)
-        mixed = returned[0, columns, :].T.astype(jnp.float32)
-        gate_out[:, columns] = (grad_ref[:, columns].astype(jnp.float32) * mixed).astype(
-            jnp.bfloat16
-        )
-        signal_out[:, columns] = returned[1, columns, :].T
-        filter_out[:, columns] = returned[2, columns, :].T
-
     for chunk in range(chunks):
 
         def drain(step, carry, chunk=chunk):
@@ -490,6 +504,51 @@
             return carry
 
         lax.fori_loop(1, groups, drain, 0)
+
+
+def tokens_kernel(
+    returned_hbm,
+    grad_hbm,
+    signal_out,
+    gate_out,
+    filter_out,
+    returned,
+    grad_ref,
+    staged,
+    load_sems,
+    sems,
+):
+    outs = (signal_out, gate_out, filter_out)
+    copies = []
+    spans = [slice(first, first + LANES) for first in range(0, grad_ref.shape[1], LANES)]
+    grad_load = pltpu.make_async_copy(grad_hbm, grad_ref, load_sems.at[len(spans)])
+    grad_load.start()
+    loads = [
+        pltpu.make_async_copy(
+            returned_hbm.at[:, columns, :], returned.at[:, columns, :], load_sems.at[block]
+        )
+        for block, columns in enumerate(spans)
+    ]
+    for load in loads:
+        load.start()
+    grad_load.wait()
+    for block, columns in enumerate(spans):
+        loads[block].wait()
+        mixed = returned[0, columns, :].T.astype(jnp.float32)
+        staged[0, :, columns] = returned[1, columns, :].T
+        staged[1, :, columns] = (grad_ref[:, columns].astype(jnp.float32) * mixed).astype(
+            jnp.bfloat16
+        )
+        staged[2, :, columns] = returned[2, columns, :].T
+        for u in range(3):
+            copies.append(
+                pltpu.make_async_copy(
+                    staged.at[u, :, columns], outs[u].at[:, columns], sems.at[block, u]
+                )
+            )
+            copies[-1].start()
+    for copy in copies:
+        copy.wait()
 
 
 def per_device_fused(signal, gate_values, filter_taps, skip_gain, grad_output):
@@ -499,19 +558,27 @@
     own = channels // groups
     chunks = own // CHUNK
     twist, inner = fused_tables(groups, seq_rows)
-    vmem = pl.BlockSpec(memory_space=pltpu.VMEM)
-    shape = jax.ShapeDtypeStruct((seq_rows, channels), jnp.bfloat16)
+    far = pl.BlockSpec(memory_space=pl.ANY)
     rows = (groups + 1, 3, CHUNK, 2 * seq_rows)
-    return pl.pallas_call(
+    operands = (
+        signal,
+        gate_values,
+        filter_taps,
+        skip_gain[None, :],
+        grad_output,
+        jnp.asarray(twist),
+        jnp.asarray(inner),
+    )
+    returned = pl.pallas_call(
         functools.partial(fused_kernel, groups, narrow_count, groups * seq_rows),
-        out_shape=(shape, shape, shape),
-        in_specs=[vmem] * 7,
-        out_specs=(vmem, vmem, vmem),
+        out_shape=jax.ShapeDtypeStruct((3, channels, seq_rows), jnp.bfloat16),
+        in_specs=[far] * len(operands),
+        out_specs=far,
         scratch_shapes=[
+            *[pltpu.VMEM(operand.shape, operand.dtype) for operand in operands],
             pltpu.VMEM((3, channels, seq_rows), jnp.bfloat16),
             pltpu.VMEM((groups, 3, own, seq_rows), jnp.bfloat16),
             pltpu.VMEM((groups, 3, own, seq_rows), jnp.bfloat16),
-            pltpu.VMEM((3, channels, seq_rows), jnp.bfloat16),
             pltpu.VMEM(rows, jnp.bfloat16),
             pltpu.VMEM(rows, jnp.bfloat16),
             pltpu.VMEM(rows, jnp.float32),
@@ -520,19 +587,27 @@
             pltpu.SemaphoreType.DMA((chunks, groups)),
             pltpu.SemaphoreType.DMA((chunks, groups)),
             pltpu.SemaphoreType.DMA,
+            pltpu.SemaphoreType.DMA((len(operands),)),
         ],
         compiler_params=pltpu.CompilerParams(
-            collective_id=0, has_side_effects=True, vmem_limit_bytes=40 * 1024 * 1024
+            collective_id=0, has_side_effects=True, vmem_limit_bytes=56 * 1024 * 1024
         ),
-    )(
-        signal,
-        gate_values,
-        filter_taps,
-        skip_gain[None, :],
-        grad_output,
-        jnp.asarray(twist),
-        jnp.asarray(inner),
-    )
+    )(*operands)
+    shape = jax.ShapeDtypeStruct((seq_rows, channels), jnp.bfloat16)
+    return pl.pallas_call(
+        tokens_kernel,
+        out_shape=(shape, shape, shape),
+        in_specs=[far, far],
+        out_specs=(far, far, far),
+        scratch_shapes=[
+            pltpu.VMEM((3, channels, seq_rows), jnp.bfloat16),
+            pltpu.VMEM((seq_rows, channels), jnp.bfloat16),
+            pltpu.VMEM((3, seq_rows, channels), jnp.bfloat16),
+            pltpu.SemaphoreType.DMA((channels // LANES + 1,)),
+            pltpu.SemaphoreType.DMA((channels // LANES, 3)),
+        ],
+        compiler_params=pltpu.CompilerParams(vmem_limit_bytes=56 * 1024 * 1024),
+    )(returned, grad_output)
 
 
 def per_device(signal, gate_values, filter_taps, skip_gain, grad_output):

time: 43.8 us -> 36.9 us (0.84)
  local copies, waits for them, and re-layouts: 8.22 us -> 0 us
  Pallas kernels: 34.6 us -> 36.1 us
    unnamed x17 -> x0, local copies, waits for them, and re-layouts: 8.22 us -> none
    pallas_call x0 -> x1, Pallas kernels: none -> 2.39 us  [per_device_fused(): pl.pallas_call(tokens_kernel, out_shape=(shape, shape, shape), in_specs=[...]
    pallas_call x1, Pallas kernels: 34.6 us -> 33.7 us  [per_device_fused(): pl.pallas_call(functools.partial(fused_kernel, groups, narrow_count, grou...]
where the time goes in v1:
time: 36.9 us; the launch traced here: 36.7 us
  Pallas kernels  36.1 us (98%)
  between operations  0.64 us (2%)
    pallas_call x1, Pallas kernels, per_device_fused(): pl.pallas_call(functools.partial(fused_kernel, groups, narrow_count, grou...  33.7 us
    pallas_call x1, Pallas kernels, per_device_fused(): pl.pallas_call(tokens_kernel, out_shape=(shape, shape, shape), in_specs=[...  2.39 us

profile of v1, /device:TPU:0, one launch (start us, length us, event | category | flops | bytes accessed | tf_op | source)
XLA Modules:
  0.0 36.7 jit_solution(631451875331666919)
XLA Ops:
  0.6 33.7 %shard_map.94.returned_hbm = bf16[3,768,128]{2,1,0:T(8,128)(2,1)} custom-call(bf16[128,768]{1,0:T(8,128)(2,1)} %signal_hbm.1, bf16[128,768]{1,0:T(8,128)(2,1)} %gate_hbm.1, bf16[128,768]{1,0:T(8,128)(2,1)} %taps_hbm.1, f32[1,48]{1,0:T(1,128)} %bitcast.1, bf16[128,768]{1,0:T(8,128)(2,1)} %grad_hbm.3, f32[4,17,128]{2,1,0:T(8,128)} %constant.4.clone.twist_hbm, ...), custom_call_target="tpu_custom_call" | custom-call | tf_op jit(solution)/shard_map/pallas_call | solution.py:572
  34.4 2.4 %shard_map.95 = (bf16[128,768]{1,0:T(8,128)(2,1)}, bf16[128,768]{1,0:T(8,128)(2,1)}, bf16[128,768]{1,0:T(8,128)(2,1)}) custom-call(bf16[3,768,128]{2,1,0:T(8,128)(2,1)} %shard_map.94.returned_hbm, bf16[128,768]{1,0:T(8,128)(2,1)} %grad_hbm.3), custom_call_target="tpu_custom_call" | custom-call | tf_op jit(solution)/shard_map/pallas_call | solution.py:597

commit v2 on v1

--- a/solution.py
+++ b/solution.py
@@ -296,6 +296,8 @@
     out_recv,
     back_send,
     back_recv,
+    pass_send,
+    pass_recv,
     local_sem,
     load_sem,
 ):
@@ -304,6 +306,7 @@
     chunks = own // CHUNK
     part = lax.axis_index("parts")
     me = lax.axis_index("wide") * narrow_count + lax.axis_index("narrow")
+    twin = (1 - part, me // narrow_count, me % narrow_count)
 
     def device(index):
         return (part, index // narrow_count, index % narrow_count)
@@ -331,17 +334,7 @@
         return carry
 
     lax.fori_loop(1, groups, greet, 0)
-
-    for load in loads[:4]:
-        load.wait()
-    for first in range(0, channels, LANES):
-        columns = slice(first, first + LANES)
-        grad_vals = grad_ref[:, columns].astype(jnp.float32)
-        inner = (grad_vals * gate_ref[:, columns].astype(jnp.float32)).astype(jnp.bfloat16)
-        outgoing[0, columns, :] = signal_ref[:, columns].T
-        outgoing[1, columns, :] = taps_ref[:, columns].T
-        outgoing[2, columns, :] = inner.T
-    pl.semaphore_wait(barrier, groups - 1)
+    pl.semaphore_signal(barrier, inc=1, device_id=twin, device_id_type=MESH)
 
     def rows_of(index, chunk):
         return pl.ds(pl.multiple_of(index * own + chunk * CHUNK, CHUNK), CHUNK)
@@ -349,16 +342,59 @@
     def chunk_rows(chunk):
         return pl.ds(pl.multiple_of(chunk * CHUNK, CHUNK), CHUNK)
 
-    def spread(chunk, step):
+    def own_rows(index):
+        return pl.ds(pl.multiple_of(index * own, CHUNK), own)
+
+    def spread_whole(u, step):
         other = (me + step) % groups
         return pltpu.make_async_remote_copy(
-            src_ref=outgoing.at[:, rows_of(other, chunk), :],
-            dst_ref=arrived.at[me, :, chunk_rows(chunk), :],
-            send_sem=out_send.at[chunk, step],
-            recv_sem=out_recv.at[chunk, step],
+            src_ref=outgoing.at[u, own_rows(other), :],
+            dst_ref=arrived.at[me, u],
+            send_sem=out_send.at[u, step],
+            recv_sem=out_recv.at[u, step],
             device_id=device(other),
             device_id_type=MESH,
         )
+
+    def spread_inner(chunk, step):
+        other = (me + step) % groups
+        return pltpu.make_async_remote_copy(
+            src_ref=outgoing.at[2, rows_of(other, chunk), :],
+            dst_ref=arrived.at[me, 2, chunk_rows(chunk), :],
+            send_sem=out_send.at[2 + chunk, step],
+            recv_sem=out_recv.at[2 + chunk, step],
+            device_id=device(other),
+            device_id_type=MESH,
+        )
+
+    def pass_on(source):
+        return pltpu.make_async_remote_copy(
+            src_ref=arrived.at[source, 1],
+            dst_ref=arrived.at[source, 1],
+            send_sem=pass_send.at[source],
+            recv_sem=pass_recv.at[source],
+            device_id=twin,
+            device_id_type=MESH,
+        )
+
+    def for_others(action):
+        def body(step, carry):
+            action(step)
+            return carry
+
+        lax.fori_loop(1, groups, body, 0)
+
+    def for_sources(parity, action):
+        def body(i, carry):
+            source = 2 * i + parity
+
+            @pl.when(source != me)
+            def _():
+                action(source)
+
+            return carry
+
+        lax.fori_loop(0, groups // 2, body, 0)
 
     def bring(chunk, step):
         other = (me + step) % groups
@@ -371,13 +407,28 @@
             device_id_type=MESH,
         )
 
+    spans = [slice(first, first + LANES) for first in range(0, channels, LANES)]
+    loads[0].wait()
+    for columns in spans:
+        outgoing[0, columns, :] = signal_ref[:, columns].T
+    pl.semaphore_wait(barrier, groups)
+    for_others(lambda step: spread_whole(0, step).start())
+    loads[1].wait()
+    for columns in spans:
+        outgoing[1, columns, :] = taps_ref[:, columns].T
+
+    @pl.when(me % 2 == part)
+    def _():
+        for_others(lambda step: spread_whole(1, step).start())
+
+    loads[2].wait()
+    loads[3].wait()
+    for columns in spans:
+        grad_vals = grad_ref[:, columns].astype(jnp.float32)
+        inner = (grad_vals * gate_ref[:, columns].astype(jnp.float32)).astype(jnp.bfloat16)
+        outgoing[2, columns, :] = inner.T
     for chunk in range(chunks):
-
-        def start(step, carry, chunk=chunk):
-            spread(chunk, step).start()
-            return carry
-
-        lax.fori_loop(1, groups, start, 0)
+        for_others(lambda step, chunk=chunk: spread_inner(chunk, step).start())
     keep = pltpu.make_async_copy(
         outgoing.at[:, pl.ds(pl.multiple_of(me * own, CHUNK), own), :],
         arrived.at[me],
@@ -396,6 +447,14 @@
     )
     keep.wait()
 
+    def take_taps(source):
+        spread_whole(1, (me - source + groups) % groups).wait_recv()
+        pass_on(source).start()
+
+    for_sources(part, take_taps)
+    for_others(lambda step: spread_whole(0, step).wait_recv())
+    for_sources(1 - part, lambda source: pass_on(source).wait_recv())
+
     kept = groups + 1
     size = kept * 3 * CHUNK
 
@@ -417,12 +476,7 @@
 
     for chunk in range(chunks):
         rows = slice(chunk * CHUNK, (chunk + 1) * CHUNK)
-
-        def await_in(step, carry, chunk=chunk):
-            spread(chunk, step).wait_recv()
-            return carry
-
-        lax.fori_loop(1, groups, await_in, 0)
+        for_others(lambda step, chunk=chunk: spread_inner(chunk, step).wait_recv())
 
         def ahead(u, carry, rows=rows):
             blocks = [arrived[a, u, rows, :].astype(jnp.float32) for a in range(groups)]
@@ -496,14 +550,16 @@
 
         lax.fori_loop(1, groups, finish, 0)
 
+    for_others(lambda step: spread_whole(0, step).wait_send())
+
+    @pl.when(me % 2 == part)
+    def _():
+        for_others(lambda step: spread_whole(1, step).wait_send())
+
+    for_sources(part, lambda source: pass_on(source).wait_send())
     for chunk in range(chunks):
-
-        def drain(step, carry, chunk=chunk):
-            spread(chunk, step).wait_send()
-            bring(chunk, step).wait_send()
-            return carry
-
-        lax.fori_loop(1, groups, drain, 0)
+        for_others(lambda step, chunk=chunk: spread_inner(chunk, step).wait_send())
+        for_others(lambda step, chunk=chunk: bring(chunk, step).wait_send())
 
 
 def tokens_kernel(
@@ -582,10 +638,12 @@
             pltpu.VMEM(rows, jnp.bfloat16),
             pltpu.VMEM(rows, jnp.bfloat16),
             pltpu.VMEM(rows, jnp.float32),
+            pltpu.SemaphoreType.DMA((2 + chunks, groups)),
+            pltpu.SemaphoreType.DMA((2 + chunks, groups)),
             pltpu.SemaphoreType.DMA((chunks, groups)),
             pltpu.SemaphoreType.DMA((chunks, groups)),
-            pltpu.SemaphoreType.DMA((chunks, groups)),
-            pltpu.SemaphoreType.DMA((chunks, groups)),
+            pltpu.SemaphoreType.DMA((groups,)),
+            pltpu.SemaphoreType.DMA((groups,)),
             pltpu.SemaphoreType.DMA,
             pltpu.SemaphoreType.DMA((len(operands),)),
         ],
@@ -615,6 +673,7 @@
     seq_rows, channels = signal.shape
     own = channels // groups
     fits = groups <= 32 and groups % 4 == 0 and seq_rows == LANES
+    fits = fits and lax.axis_size("parts") == 2
     if fits and own >= CHUNK and own % CHUNK == 0 and channels % LANES == 0:
         return per_device_fused(signal, gate_values, filter_taps, skip_gain, grad_output)
     return per_device_plain(signal, gate_values, filter_taps, skip_gain, grad_output)

time: 36.9 us -> 42.1 us (1.14); the launches traced: 36.7 us -> 41.4 us
  Pallas kernels: 36.1 us -> 40.8 us
    pallas_call x1, Pallas kernels: 33.7 us -> 38.4 us  [per_device_fused(): pl.pallas_call(functools.partial(fused_kernel, groups, narrow_count, grou...]
where the time goes in v2:
time: 42.1 us; the launch traced here: 41.4 us
  Pallas kernels  40.8 us (97%)
  between operations  0.64 us (2%)
    pallas_call x1, Pallas kernels, per_device_fused(): pl.pallas_call(functools.partial(fused_kernel, groups, narrow_count, grou...  38.4 us
    pallas_call x1, Pallas kernels, per_device_fused(): pl.pallas_call(tokens_kernel, out_shape=(shape, shape, shape), in_specs=[...  2.39 us

profile of v2, /device:TPU:0, one launch (start us, length us, event | category | flops | bytes accessed | tf_op | source)
XLA Modules:
  0.0 41.4 jit_solution(13157556872703459073)
XLA Ops:
  0.6 38.4 %shard_map.94.returned_hbm = bf16[3,768,128]{2,1,0:T(8,128)(2,1)} custom-call(bf16[128,768]{1,0:T(8,128)(2,1)} %signal_hbm.1, bf16[128,768]{1,0:T(8,128)(2,1)} %gate_hbm.1, bf16[128,768]{1,0:T(8,128)(2,1)} %taps_hbm.1, f32[1,48]{1,0:T(1,128)} %bitcast.1, bf16[128,768]{1,0:T(8,128)(2,1)} %grad_hbm.3, f32[4,17,128]{2,1,0:T(8,128)} %constant.4.clone.twist_hbm, ...), custom_call_target="tpu_custom_call" | custom-call | tf_op jit(solution)/shard_map/pallas_call | solution.py:628
  39.1 2.4 %shard_map.95 = (bf16[128,768]{1,0:T(8,128)(2,1)}, bf16[128,768]{1,0:T(8,128)(2,1)}, bf16[128,768]{1,0:T(8,128)(2,1)}) custom-call(bf16[3,768,128]{2,1,0:T(8,128)(2,1)} %shard_map.94.returned_hbm, bf16[128,768]{1,0:T(8,128)(2,1)} %grad_hbm.3), custom_call_target="tpu_custom_call" | custom-call | tf_op jit(solution)/shard_map/pallas_call | solution.py:655

commit v3 on v2

--- a/solution.py
+++ b/solution.py
@@ -345,34 +345,34 @@
     def own_rows(index):
         return pl.ds(pl.multiple_of(index * own, CHUNK), own)
 
-    def spread_whole(u, step):
+    def spread_pair(chunk, step):
         other = (me + step) % groups
         return pltpu.make_async_remote_copy(
-            src_ref=outgoing.at[u, own_rows(other), :],
-            dst_ref=arrived.at[me, u],
-            send_sem=out_send.at[u, step],
-            recv_sem=out_recv.at[u, step],
+            src_ref=outgoing.at[0:2, rows_of(other, chunk), :],
+            dst_ref=arrived.at[me, 0:2, chunk_rows(chunk), :],
+            send_sem=out_send.at[chunk, step],
+            recv_sem=out_recv.at[chunk, step],
             device_id=device(other),
             device_id_type=MESH,
         )
 
-    def spread_inner(chunk, step):
+    def spread_taps(chunk, step):
         other = (me + step) % groups
         return pltpu.make_async_remote_copy(
             src_ref=outgoing.at[2, rows_of(other, chunk), :],
             dst_ref=arrived.at[me, 2, chunk_rows(chunk), :],
-            send_sem=out_send.at[2 + chunk, step],
-            recv_sem=out_recv.at[2 + chunk, step],
+            send_sem=out_send.at[chunks + chunk, step],
+            recv_sem=out_recv.at[chunks + chunk, step],
             device_id=device(other),
             device_id_type=MESH,
         )
 
-    def pass_on(source):
+    def pass_on(chunk, source):
         return pltpu.make_async_remote_copy(
-            src_ref=arrived.at[source, 1],
-            dst_ref=arrived.at[source, 1],
-            send_sem=pass_send.at[source],
-            recv_sem=pass_recv.at[source],
+            src_ref=arrived.at[source, 2, chunk_rows(chunk), :],
+            dst_ref=arrived.at[source, 2, chunk_rows(chunk), :],
+            send_sem=pass_send.at[chunk, source],
+            recv_sem=pass_recv.at[chunk, source],
             device_id=twin,
             device_id_type=MESH,
         )
@@ -408,27 +408,22 @@
         )
 
     spans = [slice(first, first + LANES) for first in range(0, channels, LANES)]
-    loads[0].wait()
-    for columns in spans:
-        outgoing[0, columns, :] = signal_ref[:, columns].T
-    pl.semaphore_wait(barrier, groups)
-    for_others(lambda step: spread_whole(0, step).start())
-    loads[1].wait()
-    for columns in spans:
-        outgoing[1, columns, :] = taps_ref[:, columns].T
-
-    @pl.when(me % 2 == part)
-    def _():
-        for_others(lambda step: spread_whole(1, step).start())
-
-    loads[2].wait()
-    loads[3].wait()
+    for load in loads[:4]:
+        load.wait()
     for columns in spans:
         grad_vals = grad_ref[:, columns].astype(jnp.float32)
         inner = (grad_vals * gate_ref[:, columns].astype(jnp.float32)).astype(jnp.bfloat16)
-        outgoing[2, columns, :] = inner.T
+        outgoing[0, columns, :] = signal_ref[:, columns].T
+        outgoing[1, columns, :] = inner.T
+        outgoing[2, columns, :] = taps_ref[:, columns].T
+    pl.semaphore_wait(barrier, groups)
     for chunk in range(chunks):
-        for_others(lambda step, chunk=chunk: spread_inner(chunk, step).start())
+
+        @pl.when(me % 2 == part)
+        def _(chunk=chunk):
+            for_others(lambda step: spread_taps(chunk, step).start())
+
+        for_others(lambda step, chunk=chunk: spread_pair(chunk, step).start())
     keep = pltpu.make_async_copy(
         outgoing.at[:, pl.ds(pl.multiple_of(me * own, CHUNK), own), :],
         arrived.at[me],
@@ -447,13 +442,11 @@
     )
     keep.wait()
 
-    def take_taps(source):
-        spread_whole(1, (me - source + groups) % groups).wait_recv()
-        pass_on(source).start()
-
-    for_sources(part, take_taps)
-    for_others(lambda step: spread_whole(0, step).wait_recv())
-    for_sources(1 - part, lambda source: pass_on(source).wait_recv())
+    def take_taps(chunk, source):
+        spread_taps(chunk, (me - source + groups) % groups).wait_recv()
+        pass_on(chunk, source).start()
+
+    for_sources(part, functools.partial(take_taps, 0))
 
     kept = groups + 1
     size = kept * 3 * CHUNK
@@ -476,7 +469,8 @@
 
     for chunk in range(chunks):
         rows = slice(chunk * CHUNK, (chunk + 1) * CHUNK)
-        for_others(lambda step, chunk=chunk: spread_inner(chunk, step).wait_recv())
+        for_others(lambda step, chunk=chunk: spread_pair(chunk, step).wait_recv())
+        for_sources(1 - part, lambda source, chunk=chunk: pass_on(chunk, source).wait_recv())
 
         def ahead(u, carry, rows=rows):
             blocks = [arrived[a, u, rows, :].astype(jnp.float32) for a in range(groups)]
@@ -495,13 +489,15 @@
             parts = [
                 (spec_ref[k, u, :, :seq_rows], spec_ref[k, u, :, seq_rows:]) for u in range(3)
             ]
-            (s_re, s_im), (t_re, t_im), (i_re, i_im) = parts
+            (s_re, s_im), (i_re, i_im), (t_re, t_im) = parts
             store_pair(k, 0, s_re * t_re - s_im * t_im, s_re * t_im + s_im * t_re)
             store_pair(k, 1, i_re * t_re + i_im * t_im, i_im * t_re - i_re * t_im)
             store_pair(k, 2, i_re * s_re + i_im * s_im, i_im * s_re - i_re * s_im)
             return carry
 
         lax.fori_loop(0, kept, multiply, 0)
+        if chunk + 1 < chunks:
+            for_sources(part, functools.partial(take_taps, chunk + 1))
         inner_transform(2)
 
         gain = gain_all[rows, :]
@@ -514,7 +510,7 @@
                 real.append(re * cos - im * sin)
                 imag.append(im * cos + re * sin)
             for a, block in enumerate(outer_inverse(real, imag)):
-                skipped = arrived[a, 2 * u, rows, :].astype(jnp.float32)
+                skipped = arrived[a, u, rows, :].astype(jnp.float32)
                 results[a, u, rows, :] = (block + gain * skipped).astype(jnp.bfloat16)
             return carry
 
@@ -550,15 +546,14 @@
 
         lax.fori_loop(1, groups, finish, 0)
 
-    for_others(lambda step: spread_whole(0, step).wait_send())
-
-    @pl.when(me % 2 == part)
-    def _():
-        for_others(lambda step: spread_whole(1, step).wait_send())
-
-    for_sources(part, lambda source: pass_on(source).wait_send())
     for chunk in range(chunks):
-        for_others(lambda step, chunk=chunk: spread_inner(chunk, step).wait_send())
+        for_others(lambda step, chunk=chunk: spread_pair(chunk, step).wait_send())
+
+        @pl.when(me % 2 == part)
+        def _(chunk=chunk):
+            for_others(lambda step: spread_taps(chunk, step).wait_send())
+
+        for_sources(part, lambda source, chunk=chunk: pass_on(chunk, source).wait_send())
         for_others(lambda step, chunk=chunk: bring(chunk, step).wait_send())
 
 
@@ -638,12 +633,12 @@
             pltpu.VMEM(rows, jnp.bfloat16),
             pltpu.VMEM(rows, jnp.bfloat16),
             pltpu.VMEM(rows, jnp.float32),
-            pltpu.SemaphoreType.DMA((2 + chunks, groups)),
-            pltpu.SemaphoreType.DMA((2 + chunks, groups)),
+            pltpu.SemaphoreType.DMA((2 * chunks, groups)),
+            pltpu.SemaphoreType.DMA((2 * chunks, groups)),
             pltpu.SemaphoreType.DMA((chunks, groups)),
             pltpu.SemaphoreType.DMA((chunks, groups)),
-            pltpu.SemaphoreType.DMA((groups,)),
-            pltpu.SemaphoreType.DMA((groups,)),
+            pltpu.SemaphoreType.DMA((chunks, groups)),
+            pltpu.SemaphoreType.DMA((chunks, groups)),
             pltpu.SemaphoreType.DMA,
             pltpu.SemaphoreType.DMA((len(operands),)),
         ],

time: 42.1 us -> 38.3 us (0.910); the launches traced: 41.4 us -> 38.1 us
  Pallas kernels: 40.8 us -> 37.5 us
    pallas_call x1, Pallas kernels: 38.4 us -> 35.1 us  [per_device_fused(): pl.pallas_call(functools.partial(fused_kernel, groups, narrow_count, grou...]
where the time goes in v3:
time: 38.3 us; the launch traced here: 38.1 us
  Pallas kernels  37.5 us (98%)
  between operations  0.64 us (2%)
    pallas_call x1, Pallas kernels, per_device_fused(): pl.pallas_call(functools.partial(fused_kernel, groups, narrow_count, grou...  35.1 us
    pallas_call x1, Pallas kernels, per_device_fused(): pl.pallas_call(tokens_kernel, out_shape=(shape, shape, shape), in_specs=[...  2.39 us

profile of v3, /device:TPU:0, one launch (start us, length us, event | category | flops | bytes accessed | tf_op | source)
XLA Modules:
  0.0 38.1 jit_solution(14691121578363198075)
XLA Ops:
  0.6 35.1 %shard_map.94.returned_hbm = bf16[3,768,128]{2,1,0:T(8,128)(2,1)} custom-call(bf16[128,768]{1,0:T(8,128)(2,1)} %signal_hbm.1, bf16[128,768]{1,0:T(8,128)(2,1)} %gate_hbm.1, bf16[128,768]{1,0:T(8,128)(2,1)} %taps_hbm.1, f32[1,48]{1,0:T(1,128)} %bitcast.1, bf16[128,768]{1,0:T(8,128)(2,1)} %grad_hbm.3, f32[4,17,128]{2,1,0:T(8,128)} %constant.4.clone.twist_hbm, ...), custom_call_target="tpu_custom_call" | custom-call | tf_op jit(solution)/shard_map/pallas_call | solution.py:623
  35.7 2.4 %shard_map.95 = (bf16[128,768]{1,0:T(8,128)(2,1)}, bf16[128,768]{1,0:T(8,128)(2,1)}, bf16[128,768]{1,0:T(8,128)(2,1)}) custom-call(bf16[3,768,128]{2,1,0:T(8,128)(2,1)} %shard_map.94.returned_hbm, bf16[128,768]{1,0:T(8,128)(2,1)} %grad_hbm.3), custom_call_target="tpu_custom_call" | custom-call | tf_op jit(solution)/shard_map/pallas_call | solution.py:650

commit v4 on v1

--- a/solution.py
+++ b/solution.py
@@ -374,7 +374,7 @@
     for chunk in range(chunks):
 
         def start(step, carry, chunk=chunk):
-            spread(chunk, step).start()
+            spread(chunk, (step + groups // 2 - 2) % (groups - 1) + 1).start()
             return carry
 
         lax.fori_loop(1, groups, start, 0)
@@ -476,7 +476,7 @@
             results[a, 2, rows, :] = scaled.astype(jnp.bfloat16)
 
         def start_back(step, carry, chunk=chunk):
-            bring(chunk, step).start()
+            bring(chunk, (step + groups // 2 - 2) % (groups - 1) + 1).start()
             return carry
 
         lax.fori_loop(1, groups, start_back, 0)

time: 36.9 us -> 38.5 us (1.043)
  Pallas kernels: 36.1 us -> 37.7 us
    pallas_call x1, Pallas kernels: 33.7 us -> 35.3 us  [per_device_fused(): pl.pallas_call(functools.partial(fused_kernel, groups, narrow_count, grou...]
where the time goes in v4:
time: 38.5 us; the launch traced here: 38.3 us
  Pallas kernels  37.7 us (98%)
  between operations  0.64 us (2%)
    pallas_call x1, Pallas kernels, per_device_fused(): pl.pallas_call(functools.partial(fused_kernel, groups, narrow_count, grou...  35.3 us
    pallas_call x1, Pallas kernels, per_device_fused(): pl.pallas_call(tokens_kernel, out_shape=(shape, shape, shape), in_specs=[...  2.39 us

profile of v4, /device:TPU:0, one launch (start us, length us, event | category | flops | bytes accessed | tf_op | source)
XLA Modules:
  0.0 38.3 jit_solution(17965283740963062665)
XLA Ops:
  0.6 35.3 %shard_map.94.returned_hbm = bf16[3,768,128]{2,1,0:T(8,128)(2,1)} custom-call(bf16[128,768]{1,0:T(8,128)(2,1)} %signal_hbm.1, bf16[128,768]{1,0:T(8,128)(2,1)} %gate_hbm.1, bf16[128,768]{1,0:T(8,128)(2,1)} %taps_hbm.1, f32[1,48]{1,0:T(1,128)} %bitcast.1, bf16[128,768]{1,0:T(8,128)(2,1)} %grad_hbm.3, f32[4,17,128]{2,1,0:T(8,128)} %constant.4.clone.twist_hbm, ...), custom_call_target="tpu_custom_call" | custom-call | tf_op jit(solution)/shard_map/pallas_call | solution.py:572
  35.9 2.4 %shard_map.95 = (bf16[128,768]{1,0:T(8,128)(2,1)}, bf16[128,768]{1,0:T(8,128)(2,1)}, bf16[128,768]{1,0:T(8,128)(2,1)}) custom-call(bf16[3,768,128]{2,1,0:T(8,128)(2,1)} %shard_map.94.returned_hbm, bf16[128,768]{1,0:T(8,128)(2,1)} %grad_hbm.3), custom_call_target="tpu_custom_call" | custom-call | tf_op jit(solution)/shard_map/pallas_call | solution.py:597
